TPU v7x, 128 devices: a whole 4x4x4 slice. The times are simulated.
128 devices in a mesh: dp: 8 (over z, x_lo), seq: 16 (over x_hi, y, core).
Axes of the slice: x: 4 (x_hi: 2, x_lo: 2; x = x_hi * 2 + x_lo), y: 4, z: 4, core: 2. Of those that a mesh axis runs over, the one named last changes fastest.
Arguments:
- tokens: bfloat16 [8, 16384, 2048], P('dp', 'seq'), may hold values from -6 to 6
- gate: bfloat16 [8, 16384, 2048], P('dp', 'seq'), may hold values from -6 to 6
- cotangent: bfloat16 [8, 16384, 2048], P('dp', 'seq'), may hold values from -6 to 6
- first_factor: bfloat16 [32, 512, 512], P('seq'), may hold values from -0.25 to 0.25
- second_factor: bfloat16 [512, 32, 32], P('seq'), may hold values from -1 to 1
Outputs:
- input_grad: bfloat16 [8, 16384, 2048], P('dp', 'seq')
- gate_grad: bfloat16 [8, 16384, 2048], P('dp', 'seq')
- first_grad: float32 [32, 512, 512], P('seq', 'dp')
- second_grad: float32 [512, 32, 32], P('seq', 'dp')
All inputs are finite; a program needn't handle non-finite values.
Results may differ from a plain program's by a relative error of at most 0.0057.
Values may be sent and summed in bfloat16 or wider, within the bound.
A program may use at most 128 MiB of HBM per device.

v0:
```python
import jax
import jax.numpy as jnp
from jax import lax
from jax.sharding import PartitionSpec as P


def local(tokens, gate, cotangent, first_factor, second_factor):
    seqs, rows, width = tokens.shape
    dp_count = lax.axis_size("dp")
    local_blocks, block = (first_factor.shape[0], first_factor.shape[1])
    local_offsets, nblocks = (second_factor.shape[0], second_factor.shape[1])
    factor = 1.0 / jnp.sqrt(jnp.float32(width * seqs * dp_count))
    blocks = tokens.reshape(seqs, local_blocks, block, width)
    hidden = jnp.einsum(
        "bij,nbjc->nbic", first_factor, blocks, preferred_element_type=jnp.float32
    ).astype(jnp.bfloat16)
    hidden_t = lax.all_to_all(hidden, "seq", split_axis=2, concat_axis=1, tiled=True)
    mixed = jnp.einsum(
        "ipb,nbic->nipc", second_factor, hidden_t, preferred_element_type=jnp.float32
    )
    hidden_t, mixed = (hidden_t, mixed)
    gate_t = gate.reshape(seqs, local_offsets, nblocks, width).astype(jnp.float32)
    cot_t = cotangent.reshape(seqs, local_offsets, nblocks, width).astype(jnp.float32)
    gate_grad = (cot_t * mixed).astype(jnp.bfloat16).reshape(seqs, rows, width)
    mixed_grad = (cot_t * gate_t).astype(jnp.bfloat16)
    second_terms = (
        jnp.einsum("nipc,nbic->ipb", mixed_grad, hidden_t, preferred_element_type=jnp.float32)
        * factor
    )
    hidden_grad_t = jnp.einsum(
        "ipb,nipc->nbic", second_factor, mixed_grad, preferred_element_type=jnp.float32
    ).astype(jnp.bfloat16)
    second_share = lax.psum_scatter(second_terms, "dp", scatter_dimension=1, tiled=True)
    hidden_grad = lax.all_to_all(hidden_grad_t, "seq", split_axis=1, concat_axis=2, tiled=True)
    input_grad = jnp.einsum(
        "bij,nbic->nbjc", first_factor, hidden_grad, preferred_element_type=jnp.float32
    ).astype(jnp.bfloat16)
    hidden_grad, input_grad = (hidden_grad, input_grad)
    first_terms = (
        jnp.einsum("nbic,nbjc->bij", hidden_grad, blocks, preferred_element_type=jnp.float32)
        * factor
    )
    first_share = lax.psum_scatter(first_terms, "dp", scatter_dimension=1, tiled=True)
    return (input_grad.reshape(seqs, rows, width), gate_grad, first_share, second_share)


def solution(mesh):
    placed = (
        P("dp", "seq", None),
        P("dp", "seq", None),
        P("dp", "seq", None),
        P("seq", None, None),
        P("seq", None, None),
    )
    return jax.shard_map(
        local,
        mesh=mesh,
        in_specs=placed,
        out_specs=(
            P("dp", "seq", None),
            P("dp", "seq", None),
            P("seq", "dp", None),
            P("seq", "dp", None),
        ),
        check_vma=False,
    )
```

profile of v0, /device:TPU:1, one launch (start us, length us, event | category | flops | bytes accessed | tf_op | source)
XLA Modules:
  0.0 242.0 jit_solution(580242980877380652)
XLA Ops:
  7.2 0.0 copy-start
  7.2 1.2 copy-done
  8.4 7.2 %convert_bitcast_fusion = bf16[1,2,512,2048]{2,3,1,0:T(8,128)(2,1)} fusion(bf16[2,512,2048]{2,1,0:T(8,128)(2,1)} %bitcast.52, bf16[2,512,512]{2,1,0:T(8,128)(2,1)S(1)} %copy-done), kind=kOutput, calls=%fused_computation.3 | convolution fusion | flops 2149580800 | bytes 9437184 | tf_op jit(solution)/shard_map/bij,nbjc->nbic/dot_general | solution.py:14
  15.6 11.3 %copy.25 = bf16[1,2,512,2048]{3,1,0,2:T(2,128)(2,1)} copy(bf16[1,2,512,2048]{2,3,1,0:T(8,128)(2,1)} %convert_bitcast_fusion) | data formatting | bytes 8388608 | tf_op jit(solution)/shard_map/convert_element_type | solution.py:16
  26.9 8.4 %all-to-all-start.1 = ((bf16[1,2,512,2048]{3,1,0,2:T(2,128)(2,1)}), bf16[1,2,512,2048]{3,1,0,2:T(2,128)(2,1)}, u32[]{:S(2)}, u32[]{:S(2)}) async-start(bf16[1,2,512,2048]{3,1,0,2:T(2,128)(2,1)} %copy.25), calls=%async_computation.1 | async-start | bytes 8388608 | tf_op jit(solution)/shard_map/all_to_all | solution.py:17
  35.3 0.0 copy-start.5
  35.4 5.4 %multiply_convert_fusion = bf16[1,1024,2048]{2,1,0:T(8,128)(2,1)S(1)} fusion(bf16[1,1024,2048]{2,1,0:T(8,128)(2,1)} %param.6, bf16[1,1024,2048]{2,1,0:T(8,128)(2,1)} %param.7), kind=kLoop, calls=%fused_computation.2 | loop fusion | flops 8388608 | bytes 12582912 | tf_op jit(solution)/shard_map/convert_element_type | solution.py:25
  40.8 0.0 copy-start.2
  40.8 0.0 copy-done.5
  40.8 1.3 convert_bitcast_fusion.1
  42.1 0.6 copy-done.2
  42.8 4.3 %copy.21 = bf16[1,32,32,2048]{3,2,0,1:T(8,128)(2,1)} copy(bf16[1,32,32,2048]{3,1,2,0:T(8,128)(2,1)S(1)} %convert_bitcast_fusion.1) | data formatting | bytes 8388608 | tf_op jit(solution)/shard_map/convert_element_type | solution.py:32
  47.1 43.4 %all-to-all-done.1 = bf16[1,2,512,2048]{3,1,0,2:T(2,128)(2,1)} async-done(((bf16[1,2,512,2048]{3,1,0,2:T(2,128)(2,1)}), bf16[1,2,512,2048]{3,1,0,2:T(2,128)(2,1)}, u32[]{:S(2)}, u32[]{:S(2)}) %all-to-all-start.1) | async-done | bytes 4194336 | tf_op jit(solution)/shard_map/all_to_all | solution.py:17
  90.4 13.2 %all-to-all-start = ((bf16[1,32,32,2048]{3,2,0,1:T(8,128)(2,1)}), bf16[1,32,32,2048]{3,2,0,1:T(8,128)(2,1)}, u32[]{:S(2)}, u32[]{:S(2)}) async-start(bf16[1,32,32,2048]{3,2,0,1:T(8,128)(2,1)} %copy.21), calls=%async_computation | async-start | bytes 8388608 | tf_op jit(solution)/shard_map/all_to_all | solution.py:34
  103.6 0.2 reduce-scatter.5.cloned.1.call-start
  103.8 4.1 %copy.26 = bf16[1,2,512,2048]{3,2,1,0:T(8,128)(2,1)S(1)} copy(bf16[1,2,512,2048]{3,1,0,2:T(2,128)(2,1)} %all-to-all-done.1) | data formatting | bytes 8388608 | tf_op jit(solution)/shard_map/all_to_all | solution.py:17
  107.9 6.3 %copy.27 = bf16[1,16,2,32,2048]{4,2,1,3,0:T(2,128)(2,1)} copy(bf16[1,16,2,32,2048]{4,3,1,2,0:T(8,128)(2,1)S(1)} %bitcast.48) | data formatting | bytes 8388608 | tf_op jit(solution)/shard_map/all_to_all | solution.py:17
  114.2 7.3 %reshape.75 = bf16[32,32,2048]{2,0,1:T(8,128)(2,1)} reshape(bf16[1,16,2,32,2048]{4,2,1,3,0:T(2,128)(2,1)} %copy.27) | data formatting | bytes 8388608 | tf_op jit(solution)/shard_map/reshape.11
  121.5 4.7 %convolution_multiply_fusion.1 = f32[32,32,32]{2,1,0:T(8,128)S(1)} fusion(bf16[32,32,2048]{2,1,0:T(8,128)(2,1)} %bitcast.46, bf16[32,32,2048]{2,0,1:T(8,128)(2,1)} %reshape.75), kind=kOutput, calls=%fused_computation.7 | convolution fusion | flops 134250496 | bytes 8519680 | tf_op jit(solution)/shard_map/nipc,nbic->ipb/dot_general | solution.py:27
  126.2 1.1 copy.28
  127.3 0.0 reduce-scatter.5.cloned.1.call-update
  127.3 0.3 reduce-scatter.3.cloned.1.call-start
  127.6 38.7 %all-to-all-done = bf16[1,32,32,2048]{3,2,0,1:T(8,128)(2,1)} async-done(((bf16[1,32,32,2048]{3,2,0,1:T(8,128)(2,1)}), bf16[1,32,32,2048]{3,2,0,1:T(8,128)(2,1)}, u32[]{:S(2)}, u32[]{:S(2)}) %all-to-all-start) | async-done | bytes 4194336 | tf_op jit(solution)/shard_map/all_to_all | solution.py:34
  166.3 0.0 copy-start.6
  166.3 2.7 %copy.22 = bf16[1,16,2,32,2048]{4,3,1,2,0:T(8,128)(2,1)S(1)} copy(bf16[1,16,2,32,2048]{4,3,2,1,0:T(8,128)(2,1)} %bitcast.3) | data formatting | bytes 8388608 | tf_op jit(solution)/shard_map/all_to_all | solution.py:34
  168.9 0.0 copy-start.4
  169.0 2.0 copy-done.4
  171.0 0.0 copy-done.6
  171.0 3.7 %convolution_multiply_fusion = f32[2,512,512]{2,1,0:T(8,128)} fusion(bf16[2,512,2048]{2,1,0:T(8,128)(2,1)S(1)} %bitcast.50, bf16[2,512,2048]{2,1,0:T(8,128)(2,1)S(1)} %bitcast.53), kind=kOutput, calls=%fused_computation.6 | convolution fusion | flops 2148007936 | bytes 10485760 | tf_op jit(solution)/shard_map/nbic,nbjc->bij/dot_general | solution.py:40
  174.7 0.0 reduce-scatter.3.cloned.1.call-update
  174.7 0.0 copy-start.1
  174.7 0.0 copy-start.3
  174.7 6.7 %convolution_convert_fusion = bf16[2,2048,512]{1,2,0:T(8,128)(2,1)} fusion(bf16[2,512,2048]{2,1,0:T(8,128)(2,1)} %bitcast.51, bf16[2,512,512]{2,1,0:T(8,128)(2,1)S(1)} %copy-done), kind=kOutput, calls=%fused_computation.5 | convolution fusion | flops 2149580800 | bytes 9437184 | tf_op jit(solution)/shard_map/bij,nbic->nbjc/dot_general | solution.py:35
  181.4 0.0 copy-done.1
  181.4 0.0 copy-done.3
  181.4 3.3 %fusion = bf16[1,32,32,2048]{3,2,1,0:T(8,128)(2,1)} fusion(bf16[32,32,32]{2,1,0:T(8,128)(2,1)S(1)} %copy-done.5, bf16[32,32,2048]{2,0,1:T(8,128)(2,1)S(1)} %copy-done.1, bf16[1,32,32,2048]{3,2,1,0:T(8,128)(2,1)S(1)} %bitcast.47), kind=kOutput, calls=%fused_computation.1 | convolution fusion | flops 140509184 | bytes 12648448 | tf_op jit(solution)/shard_map/ipb,nbic->nipc/dot_general | solution.py:18
  184.7 0.0 reduce-scatter.5.cloned.1.call-done
  184.7 1.5 copy.29
  186.2 49.0 %reduce-scatter.3.cloned.1.call-done = f32[2,64,512]{2,1,0:T(8,128)} async-done(((f32[2,512,512]{2,1,0:T(8,128)}), f32[2,64,512]{2,1,0:T(8,128)}) %reduce-scatter.3.cloned.1.call-update) | async-done | bytes 262160 | tf_op jit(solution)/shard_map/reduce_scatter | solution.py:43
Async XLA Ops:
  7.2 1.2 copy-start
  26.9 63.5 %all-to-all-start.1 = ((bf16[1,2,512,2048]{3,1,0,2:T(2,128)(2,1)}), bf16[1,2,512,2048]{3,1,0,2:T(2,128)(2,1)}, u32[]{:S(2)}, u32[]{:S(2)}) async-start(bf16[1,2,512,2048]{3,1,0,2:T(2,128)(2,1)} %copy.25), calls=%async_computation.1 | async-start | bytes 8388608 | tf_op jit(solution)/shard_map/all_to_all | solution.py:17
  35.3 5.5 %copy-start.5 = (bf16[32,32,32]{2,1,0:T(8,128)(2,1)S(1)}, bf16[32,32,32]{2,1,0:T(8,128)(2,1)}, u32[]{:S(2)}) copy-start(bf16[32,32,32]{2,1,0:T(8,128)(2,1)} %param.9) | copy-start | bytes 196612
  40.8 2.0 copy-start.2
  90.4 75.8 %all-to-all-start = ((bf16[1,32,32,2048]{3,2,0,1:T(8,128)(2,1)}), bf16[1,32,32,2048]{3,2,0,1:T(8,128)(2,1)}, u32[]{:S(2)}, u32[]{:S(2)}) async-start(bf16[1,32,32,2048]{3,2,0,1:T(8,128)(2,1)} %copy.21), calls=%async_computation | async-start | bytes 8388608 | tf_op jit(solution)/shard_map/all_to_all | solution.py:34
  103.6 81.1 %reduce-scatter.5.cloned.1.call-start = ((), (), s32[]{:S(2)}) async-start(), calls=%async_computation.5 | async-start | bytes 589824 | tf_op jit(solution)/shard_map/reduce_scatter | solution.py:33
  127.3 107.9 %reduce-scatter.3.cloned.1.call-start = ((), (), s32[]{:S(2)}) async-start(), calls=%async_computation.4 | async-start | bytes 2359296 | tf_op jit(solution)/shard_map/reduce_scatter | solution.py:43
  166.3 4.7 %copy-start.6 = (bf16[1,1024,2048]{2,1,0:T(8,128)(2,1)S(1)}, bf16[1,1024,2048]{2,1,0:T(8,128)(2,1)}, u32[]{:S(2)}) copy-start(bf16[1,1024,2048]{2,1,0:T(8,128)(2,1)} %param.5) | copy-start | bytes 12582916
  168.9 2.0 copy-start.4
  174.7 6.8 %copy-start.1 = (bf16[32,32,2048]{2,0,1:T(8,128)(2,1)S(1)}, bf16[32,32,2048]{2,0,1:T(8,128)(2,1)}, u32[]{:S(2)}) copy-start(bf16[32,32,2048]{2,0,1:T(8,128)(2,1)} %reshape.75) | copy-start | bytes 12582916
  174.7 6.7 %copy-start.3 = (bf16[1,1024,2048]{2,1,0:T(8,128)(2,1)S(1)}, bf16[1,1024,2048]{2,1,0:T(8,128)(2,1)}, u32[]{:S(2)}) copy-start(bf16[1,1024,2048]{2,1,0:T(8,128)(2,1)} %param.7) | copy-start | bytes 12582916
Sparse Core Ops, SparseCore 0:
  127.4 39.6 reduce-scatter.4
  174.8 60.3 reduce-scatter.2
where the time goes:
time: 243 us; the launch traced here: 242 us
  waiting for transfers between devices  131 us (54%)
  local copies, waits for them, and re-layouts  42.4 us (17%)
  matrix products  26.9 us (11%)
  starting transfers between devices  22.1 us (9%)
  between operations  14.1 us (6%)
  other arithmetic  5.43 us (2%)
    reduce_scatter x1, waiting for transfers between devices, local(): lax.psum_scatter(first_terms, 'dp', scatter_dimension=1, tiled=True)  49 us
    all_to_all x1, waiting for transfers between devices, local(): lax.all_to_all(hidden, 'seq', split_axis=2, concat_axis=1, tiled=True)  43.4 us
    all_to_all x1, waiting for transfers between devices, local(): lax.all_to_all(hidden_grad_t, 'seq', split_axis=1, concat_axis=2, tiled=T...  38.7 us
    all_to_all x1, starting transfers between devices, local(): lax.all_to_all(hidden_grad_t, 'seq', split_axis=1, concat_axis=2, tiled=T...  13.2 us
    convert_element_type x1, local copies, waits for them, and re-layouts, local(): hidden = jnp.einsum('bij,nbjc->nbic', first_factor, blocks, preferred_ele...  11.3 us
    all_to_all x2, local copies, waits for them, and re-layouts, local(): lax.all_to_all(hidden, 'seq', split_axis=2, concat_axis=1, tiled=True)  10.4 us
    all_to_all x1, starting transfers between devices, local(): lax.all_to_all(hidden, 'seq', split_axis=2, concat_axis=1, tiled=True)  8.45 us
    another operation x1, local copies, waits for them, and re-layouts  7.26 us
  transfers between devices with their start and end apart: 4, of which 3 were waited for; matrix products, arithmetic and copies ran while one was open for 22% of the time, Pallas kernels for 0%

commit v1 on v0

v1 whole, which is shorter than its diff:
```python
import functools
import math

import jax
import jax.numpy as jnp
from jax import lax
from jax.experimental import pallas as pl
from jax.experimental.pallas import tpu as pltpu
from jax.sharding import PartitionSpec as P

MESH = pl.DeviceIdType.MESH
F32, BF16 = jnp.float32, jnp.bfloat16
CHUNKS = 8
SEQ, DP = 16, 8
NB, BS, G = 32, 512, 16
NT = (((1,), (1,)), ((), ()))


def iota(shape, dim):
    return lax.broadcasted_iota(jnp.int32, shape, dim)


def kernel(
    width, scale,
    tok, gate, cot, first, second,
    ig, gg, fo, so,
    tok_v, cot_v, mg_v, f_v, ft_v, s_v, w_v, wt_v,
    hg_send, h_send, hg_recv, h_recv,
    facc, sacc, zrecv, xsend, xrecv, xkeep, sec_send, sec_recv,
    load_sem, fac_sem, hg_ss, hg_rs, h_ss, h_rs, z_ss, z_rs, x_ss, x_rs, s_ss, s_rs,
):
    cw = width // CHUNKS
    dp, me = lax.axis_index("dp"), lax.axis_index("seq")
    z, xl = dp // 2, dp % 2

    def chunk_loads(k):
        cols = pl.ds(pl.multiple_of(k * cw, cw), cw)
        return (
            pltpu.make_async_copy(cot.at[:, cols], cot_v.at[k], load_sem.at[0, k]),
            pltpu.make_async_copy(gate.at[:, cols], mg_v.at[k], load_sem.at[1, k]),
            pltpu.make_async_copy(tok.at[:, cols], tok_v.at[k], load_sem.at[2, k]),
        )

    load_second = pltpu.make_async_copy(second, s_v, fac_sem.at[0])
    load_first = pltpu.make_async_copy(first, f_v, fac_sem.at[1])
    load_second.start()

    def start_pair(k, carry):
        a, b, _ = chunk_loads(k)
        a.start()
        b.start()
        return carry

    def start_tok(k, carry):
        chunk_loads(k)[2].start()
        return carry

    lax.fori_loop(0, CHUNKS, start_pair, 0)
    load_first.start()
    lax.fori_loop(0, CHUNKS, start_tok, 0)

    barrier = pltpu.get_barrier_semaphore()

    def greet_seq(p, carry):
        pl.semaphore_signal(barrier, inc=1, device_id=(dp, (me + p) % SEQ), device_id_type=MESH)
        return carry

    def greet_dp(p, carry):
        pl.semaphore_signal(barrier, inc=1, device_id=((dp + p) % DP, me), device_id_type=MESH)
        return carry

    lax.fori_loop(1, SEQ, greet_seq, 0)
    lax.fori_loop(1, DP, greet_dp, 0)

    load_second.wait()
    n = G * NB
    spread = (iota((n, NB), 0) // G == iota((n, NB), 1)).astype(BF16)
    same = iota((n, n), 0) // NB == iota((n, n), 1) % G
    same_t = iota((n, n), 1) // NB == iota((n, n), 0) % G
    for g in range(2):
        s_g = s_v[g * n : (g + 1) * n, :]
        w = lax.dot_general(s_g, spread, NT, preferred_element_type=F32)
        w_v[g] = jnp.where(same, w, 0.0).astype(BF16)
        wt = lax.dot_general(spread, s_g, NT, preferred_element_type=F32)
        wt_v[g] = jnp.where(same_t, wt, 0.0).astype(BF16)

    def send(src, dst, k, ss, rs):
        place = dst.at[k, :, pl.ds(2 * me, 2)]

        def one(p, carry):
            t = (me + p) % SEQ
            pltpu.make_async_remote_copy(
                src_ref=src.at[k, t], dst_ref=place, send_sem=ss.at[k], recv_sem=rs.at[k],
                device_id=(dp, t), device_id_type=MESH,
            ).start()
            return carry

        lax.fori_loop(1, SEQ, one, 0)
        pltpu.make_async_copy(src.at[k, me], place, rs.at[k]).start()

    def wait_sent(src, k, ss):
        ref = src.at[k, pl.ds(0, SEQ - 1)]
        pltpu.make_async_copy(ref, ref, ss.at[k]).wait()

    def wait_all(dst, k, rs):
        pltpu.make_async_copy(dst.at[k], dst.at[k], rs.at[k]).wait()

    def make_hg(k):
        a, b, _ = chunk_loads(k)
        a.wait()
        b.wait()
        for g in range(2):
            rows = slice(g * n, (g + 1) * n)
            m = (cot_v[k, rows, :].astype(F32) * mg_v[k, rows, :].astype(F32)).astype(BF16)
            mg_v[k, rows, :] = m
            hg = jnp.dot(wt_v[g], m, preferred_element_type=F32).astype(BF16)
            hg_send[k, :, :, g] = hg.reshape(SEQ, 2, G, cw)

    make_hg(0)
    pl.semaphore_wait(barrier, SEQ - 1 + DP - 1)
    send(hg_send, hg_recv, 0, hg_ss, hg_rs)

    def hg_step(k, carry):
        make_hg(k)
        send(hg_send, hg_recv, k, hg_ss, hg_rs)
        return carry

    lax.fori_loop(1, CHUNKS, hg_step, 0)

    load_first.wait()

    def h_step(k, carry):
        chunk_loads(k)[2].wait()
        for b in range(2):
            h = jnp.dot(f_v[b], tok_v[k, b * BS : (b + 1) * BS, :], preferred_element_type=F32)
            h_send[k, :, :, b] = h.astype(BF16).reshape(SEQ, 2, G, cw)
        return carry

    lax.fori_loop(0, CHUNKS, h_step, 0)
    for b in range(2):
        ft_v[b] = f_v[b].T

    facc[...] = jnp.zeros_like(facc)
    sacc[...] = jnp.zeros_like(sacc)

    def back_step(k, carry):
        wait_sent(hg_send, k, hg_ss)
        send(h_send, h_recv, k, h_ss, h_rs)
        wait_all(hg_recv, k, hg_rs)
        cols = pl.ds(pl.multiple_of(k * cw, cw), cw)
        for b in range(2):
            hg = hg_recv[k, b].reshape(BS, cw)
            rows = slice(b * BS, (b + 1) * BS)
            ig[rows, cols] = jnp.dot(ft_v[b], hg, preferred_element_type=F32).astype(BF16)
            terms = lax.dot_general(hg, tok_v[k, rows, :], NT, preferred_element_type=F32)
            facc[b] += terms.reshape(4, 2, 64, BS)
        return carry

    lax.fori_loop(0, CHUNKS, back_step, 0)

    def z_copy(d):
        t = (z + d) % 4
        return pltpu.make_async_remote_copy(
            src_ref=facc.at[:, t], dst_ref=zrecv.at[d - 1],
            send_sem=z_ss.at[d - 1], recv_sem=z_rs.at[d - 1],
            device_id=(t * 2 + xl, me), device_id_type=MESH,
        )

    x_copy = pltpu.make_async_remote_copy(
        src_ref=xsend, dst_ref=xrecv, send_sem=x_ss, recv_sem=x_rs,
        device_id=(z * 2 + 1 - xl, me), device_id_type=MESH,
    )
    for d in (1, 2, 3):
        z_copy(d).start()

    def forth_step(k, carry):
        wait_all(h_recv, k, h_rs)
        cols = pl.ds(pl.multiple_of(k * cw, cw), cw)
        for g in range(2):
            h = h_recv[k, g].reshape(n, cw)
            rows = slice(g * n, (g + 1) * n)
            mixed = jnp.dot(w_v[g], h, preferred_element_type=F32)
            gg[rows, cols] = (cot_v[k, rows, :].astype(F32) * mixed).astype(BF16)
            sacc[g] += lax.dot_general(mg_v[k, rows, :], h, NT, preferred_element_type=F32)
        return carry

    half = CHUNKS // 2
    lax.fori_loop(0, half, forth_step, 0)

    for d in (1, 2, 3):
        z_copy(d).wait()
    for b in range(2):
        other = facc[b, z, 1 - xl] + zrecv[0, b, 1 - xl] + zrecv[1, b, 1 - xl] + zrecv[2, b, 1 - xl]
        xsend[b] = other.astype(BF16)
    x_copy.start()
    for b in range(2):
        xkeep[b] = facc[b, z, xl] + zrecv[0, b, xl] + zrecv[1, b, xl] + zrecv[2, b, xl]

    lax.fori_loop(half, CHUNKS - 1, forth_step, 0)
    x_copy.wait()
    fo[...] = (xkeep[...] + xrecv[...].astype(F32)) * scale
    forth_step(CHUNKS - 1, 0)

    high = lax.Precision.HIGHEST
    gather = (iota((n, 128), 0) // G == iota((n, 128), 1) % NB).astype(F32)
    inner = iota((n, 128), 0) % 4 == iota((n, 128), 1) // NB
    at, of = iota((128, n), 0), iota((128, n), 1)
    pick = ((at % G == of // NB) & (at // G == of % NB // 4)).astype(F32)
    for g in range(2):
        own = jnp.where(same, sacc[g], 0.0)
        wide = jnp.dot(own, gather, precision=high, preferred_element_type=F32)
        wide = jnp.where(inner, wide, 0.0)
        share = jnp.dot(pick, wide, precision=high, preferred_element_type=F32)
        sec_send[:, g] = share.reshape(DP, G, 128)

    def s_copy(p):
        t = (dp + p) % DP
        return pltpu.make_async_remote_copy(
            src_ref=sec_send.at[t], dst_ref=sec_recv.at[p - 1],
            send_sem=s_ss.at[p - 1], recv_sem=s_rs.at[p - 1],
            device_id=(t, me), device_id_type=MESH,
        )

    for p in range(1, DP):
        s_copy(p).start()

    def drain(k, carry):
        wait_sent(h_send, k, h_ss)
        return carry

    lax.fori_loop(0, CHUNKS, drain, 0)
    total = sec_send[dp]
    for p in range(1, DP):
        s_copy(p).wait()
        total = total + sec_recv[p - 1]
    so[...] = total * scale


def local(tokens, gate, cotangent, first_factor, second_factor):
    seqs, rows, width = tokens.shape
    scale = 1.0 / math.sqrt(width * seqs * DP)
    cw = width // CHUNKS
    flat = (rows, width)
    vm = pltpu.VMEM
    dma = pltpu.SemaphoreType.DMA
    out = (
        vm(flat, BF16), vm(flat, BF16), vm((2, 64, BS), F32), vm((2, G, 128), F32),
    )
    scratch = [
        vm((CHUNKS, rows, cw), BF16), vm((CHUNKS, rows, cw), BF16), vm((CHUNKS, rows, cw), BF16),
        vm((2, BS, BS), BF16), vm((2, BS, BS), BF16), vm((BS * 2, NB), BF16),
        vm((2, BS, BS), BF16), vm((2, BS, BS), BF16),
        vm((CHUNKS, SEQ, 2, 2, G, cw), BF16), vm((CHUNKS, SEQ, 2, 2, G, cw), BF16),
        vm((CHUNKS, 2, NB, G, cw), BF16), vm((CHUNKS, 2, NB, G, cw), BF16),
        vm((2, 4, 2, 64, BS), F32), vm((2, BS, BS), F32), vm((3, 2, 2, 64, BS), F32),
        vm((2, 64, BS), BF16), vm((2, 64, BS), BF16), vm((2, 64, BS), F32),
        vm((DP, 2, G, 128), F32), vm((DP - 1, 2, G, 128), F32),
        dma((3, CHUNKS)), dma((2,)),
        dma((CHUNKS,)), dma((CHUNKS,)), dma((CHUNKS,)), dma((CHUNKS,)),
        dma((3,)), dma((3,)), dma, dma, dma((DP - 1,)), dma((DP - 1,)),
    ]
    hbm = pl.BlockSpec(memory_space=pl.ANY)
    inner = pl.BlockSpec(memory_space=pltpu.VMEM)
    ig, gg, fo, so = pl.pallas_call(
        functools.partial(kernel, width, scale),
        out_shape=out,
        in_specs=[hbm] * 5,
        out_specs=[inner] * 4,
        scratch_shapes=scratch,
        compiler_params=pltpu.CompilerParams(
            collective_id=0, has_side_effects=True, vmem_limit_bytes=52 * 2**20
        ),
        cost_estimate=pl.CostEstimate(
            flops=15 * 2**30, bytes_accessed=22 * 2**20, transcendentals=0
        ),
        name="mixer",
    )(
        tokens.reshape(flat), gate.reshape(flat), cotangent.reshape(flat),
        first_factor, second_factor.reshape(BS * 2, NB),
    )
    return (
        ig.reshape(seqs, rows, width), gg.reshape(seqs, rows, width),
        fo, so.reshape(NB, 4, NB),
    )


def solution(mesh):
    placed = (
        P("dp", "seq", None),
        P("dp", "seq", None),
        P("dp", "seq", None),
        P("seq", None, None),
        P("seq", None, None),
    )
    return jax.shard_map(
        local,
        mesh=mesh,
        in_specs=placed,
        out_specs=(
            P("dp", "seq", None),
            P("dp", "seq", None),
            P("seq", "dp", None),
            P("seq", "dp", None),
        ),
        check_vma=False,
    )
```

time: 243 us -> 120 us (0.49)
  waiting for transfers between devices: 131 us -> 0 us
  Pallas kernels: 0 us -> 113 us
  local copies, waits for them, and re-layouts: 42.4 us -> 5.45 us
  matrix products: 26.9 us -> 0 us
  starting transfers between devices: 22.1 us -> 0 us
  between operations: 14.1 us -> 0.64 us
  other arithmetic: 5.43 us -> 0 us
    pallas_call x0 -> x1, Pallas kernels: none -> 113 us  [local(): pl.pallas_call(functools.partial(kernel, width, scale), out_shape=out, in...]
    all_to_all x2 -> x0, waiting for transfers between devices: 82 us -> none  [the longest x1 43.4 us: local(): lax.all_to_all(hidden, 'seq', split_axis=2, concat_axis=1, tiled=True)]
    reduce_scatter x2 -> x0, waiting for transfers between devices: 49 us -> none  [the longest x1 49 us: local(): lax.psum_scatter(first_terms, 'dp', scatter_dimension=1, tiled=True)]
    dot_general x6 -> x0, matrix products: 26.9 us -> none  [the longest x1 7.25 us: local(): jnp.einsum('bij,nbjc->nbic', first_factor, blocks, preferred_element_type...]
    all_to_all x2 -> x0, starting transfers between devices: 21.6 us -> none  [the longest x1 13.2 us: local(): lax.all_to_all(hidden_grad_t, 'seq', split_axis=1, concat_axis=2, tiled=T...]
    convert_element_type x2 -> x0, local copies, waits for them, and re-layouts: 15.6 us -> none  [the longest x1 11.3 us: local(): hidden = jnp.einsum('bij,nbjc->nbic', first_factor, blocks, preferred_ele...]
    all_to_all x3 -> x0, local copies, waits for them, and re-layouts: 13.1 us -> none  [the longest x2 10.4 us: local(): lax.all_to_all(hidden, 'seq', split_axis=2, concat_axis=1, tiled=True)]
    another operation x1 -> x0, local copies, waits for them, and re-layouts: 7.26 us -> none
  transfers between devices with their start and end apart: 4 -> 0, of which waited for: 3 -> 0; matrix products, arithmetic and copies ran while one was open for 22% -> 0% of each run, Pallas kernels for 0% -> 0%
where the time goes in v1:
time: 120 us; the launch traced here: 119 us
  Pallas kernels  113 us (94%)
  local copies, waits for them, and re-layouts  5.45 us (5%)
    pallas_call x1, Pallas kernels, local(): pl.pallas_call(functools.partial(kernel, width, scale), out_shape=out, in...  113 us
    unnamed x3, local copies, waits for them, and re-layouts  4.73 us

profile of v1, /device:TPU:1, one launch (start us, length us, event | category | flops | bytes accessed | tf_op | source)
XLA Modules:
  0.0 119.2 jit_solution(7467977308101625145)
XLA Ops:
  0.6 113.1 %mixer.1 = (bf16[1024,2048]{1,0:T(8,128)(2,1)S(1)}, bf16[1024,2048]{1,0:T(8,128)(2,1)S(1)}, f32[2,64,512]{2,1,0:T(8,128)S(1)}, f32[2,16,128]{2,1,0:T(8,128)S(1)}) custom-call(bf16[1024,2048]{1,0:T(8,128)(2,1)} %bitcast.8, bf16[1024,2048]{1,0:T(8,128)(2,1)} %bitcast.9, bf16[1024,2048]{1,0:T(8,128)(2,1)} %bitcast.10, bf16[2,512,512]{2,1,0:T(8,128)(2,1)} %first.1, ...), custom_call_target="tpu_custom_call" | custom-call | flops 16106127360 | bytes 23068672 | tf_op jit(solution)/shard_map/mixer/pallas_call | solution.py:264
  113.7 2.0 %copy.12 = bf16[1,1024,2048]{2,1,0:T(8,128)(2,1)} copy(bf16[1,1024,2048]{2,1,0:T(8,128)(2,1)S(1)} %bitcast.7) | data formatting | bytes 8388608
  115.7 2.0 %copy.13 = bf16[1,1024,2048]{2,1,0:T(8,128)(2,1)} copy(bf16[1,1024,2048]{2,1,0:T(8,128)(2,1)S(1)} %bitcast.6) | data formatting | bytes 8388608
  117.7 0.7 reshape.35
  118.5 0.7 copy.14

commit v2 on v1

--- a/solution.py
+++ b/solution.py
@@ -36,28 +36,23 @@
     def chunk_loads(k):
         cols = pl.ds(pl.multiple_of(k * cw, cw), cw)
         return (
-            pltpu.make_async_copy(cot.at[:, cols], cot_v.at[k], load_sem.at[0, k]),
-            pltpu.make_async_copy(gate.at[:, cols], mg_v.at[k], load_sem.at[1, k]),
-            pltpu.make_async_copy(tok.at[:, cols], tok_v.at[k], load_sem.at[2, k]),
-        )
+            (cot.at[:, cols], cot_v.at[k], load_sem.at[0, k]),
+            (gate.at[:, cols], mg_v.at[k], load_sem.at[1, k]),
+            (tok.at[:, cols], tok_v.at[k], load_sem.at[2, k]),
+        )
+
+    def start_loads(k, which):
+        for a in which:
+            pltpu.make_async_copy(*chunk_loads(k)[a]).start()
+
+    def wait_loads(k, which):
+        for a in which:
+            pltpu.make_async_copy(*chunk_loads(k)[a]).wait()
 
     load_second = pltpu.make_async_copy(second, s_v, fac_sem.at[0])
     load_first = pltpu.make_async_copy(first, f_v, fac_sem.at[1])
     load_second.start()
-
-    def start_pair(k, carry):
-        a, b, _ = chunk_loads(k)
-        a.start()
-        b.start()
-        return carry
-
-    def start_tok(k, carry):
-        chunk_loads(k)[2].start()
-        return carry
-
-    lax.fori_loop(0, CHUNKS, start_pair, 0)
-    load_first.start()
-    lax.fori_loop(0, CHUNKS, start_tok, 0)
+    start_loads(0, (0, 1))
 
     barrier = pltpu.get_barrier_semaphore()
 
@@ -71,6 +66,7 @@
 
     lax.fori_loop(1, SEQ, greet_seq, 0)
     lax.fori_loop(1, DP, greet_dp, 0)
+    start_loads(1, (0, 1))
 
     load_second.wait()
     n = G * NB
@@ -78,10 +74,9 @@
     same = iota((n, n), 0) // NB == iota((n, n), 1) % G
     same_t = iota((n, n), 1) // NB == iota((n, n), 0) % G
     for g in range(2):
-        s_g = s_v[g * n : (g + 1) * n, :]
-        w = lax.dot_general(s_g, spread, NT, preferred_element_type=F32)
-        w_v[g] = jnp.where(same, w, 0.0).astype(BF16)
-        wt = lax.dot_general(spread, s_g, NT, preferred_element_type=F32)
+        wt = lax.dot_general(
+            spread, s_v[g * n : (g + 1) * n, :], NT, preferred_element_type=F32
+        )
         wt_v[g] = jnp.where(same_t, wt, 0.0).astype(BF16)
 
     def send(src, dst, k, ss, rs):
@@ -106,9 +101,7 @@
         pltpu.make_async_copy(dst.at[k], dst.at[k], rs.at[k]).wait()
 
     def make_hg(k):
-        a, b, _ = chunk_loads(k)
-        a.wait()
-        b.wait()
+        wait_loads(k, (0, 1))
         for g in range(2):
             rows = slice(g * n, (g + 1) * n)
             m = (cot_v[k, rows, :].astype(F32) * mg_v[k, rows, :].astype(F32)).astype(BF16)
@@ -121,16 +114,32 @@
     send(hg_send, hg_recv, 0, hg_ss, hg_rs)
 
     def hg_step(k, carry):
+        @pl.when(k < CHUNKS - 1)
+        def _():
+            start_loads(k + 1, (0, 1))
+
         make_hg(k)
         send(hg_send, hg_recv, k, hg_ss, hg_rs)
         return carry
 
     lax.fori_loop(1, CHUNKS, hg_step, 0)
 
+    load_first.start()
+
+    def load_tok(k, carry):
+        start_loads(k, (2,))
+        return carry
+
+    lax.fori_loop(0, CHUNKS, load_tok, 0)
+    for g in range(2):
+        w = lax.dot_general(
+            s_v[g * n : (g + 1) * n, :], spread, NT, preferred_element_type=F32
+        )
+        w_v[g] = jnp.where(same, w, 0.0).astype(BF16)
     load_first.wait()
 
     def h_step(k, carry):
-        chunk_loads(k)[2].wait()
+        wait_loads(k, (2,))
         for b in range(2):
             h = jnp.dot(f_v[b], tok_v[k, b * BS : (b + 1) * BS, :], preferred_element_type=F32)
             h_send[k, :, :, b] = h.astype(BF16).reshape(SEQ, 2, G, cw)
@@ -173,15 +182,26 @@
     for d in (1, 2, 3):
         z_copy(d).start()
 
-    def forth_step(k, carry):
-        wait_all(h_recv, k, h_rs)
+    def second_terms(k):
+        for g in range(2):
+            h = h_recv[k, g].reshape(n, cw)
+            m = mg_v[k, g * n : (g + 1) * n, :]
+            terms = lax.dot_general(m, h, NT, preferred_element_type=F32)
+            terms = jnp.where(same, terms, 0.0).reshape(G, NB, n)
+            sacc[g] += jnp.sum(terms, axis=0)
+
+    def gate_part(k):
         cols = pl.ds(pl.multiple_of(k * cw, cw), cw)
         for g in range(2):
             h = h_recv[k, g].reshape(n, cw)
             rows = slice(g * n, (g + 1) * n)
             mixed = jnp.dot(w_v[g], h, preferred_element_type=F32)
             gg[rows, cols] = (cot_v[k, rows, :].astype(F32) * mixed).astype(BF16)
-            sacc[g] += lax.dot_general(mg_v[k, rows, :], h, NT, preferred_element_type=F32)
+
+    def forth_step(k, carry):
+        wait_all(h_recv, k, h_rs)
+        second_terms(k)
+        gate_part(k)
         return carry
 
     half = CHUNKS // 2
@@ -199,19 +219,11 @@
     lax.fori_loop(half, CHUNKS - 1, forth_step, 0)
     x_copy.wait()
     fo[...] = (xkeep[...] + xrecv[...].astype(F32)) * scale
-    forth_step(CHUNKS - 1, 0)
-
-    high = lax.Precision.HIGHEST
-    gather = (iota((n, 128), 0) // G == iota((n, 128), 1) % NB).astype(F32)
-    inner = iota((n, 128), 0) % 4 == iota((n, 128), 1) // NB
-    at, of = iota((128, n), 0), iota((128, n), 1)
-    pick = ((at % G == of // NB) & (at // G == of % NB // 4)).astype(F32)
+    wait_all(h_recv, CHUNKS - 1, h_rs)
+    second_terms(CHUNKS - 1)
     for g in range(2):
-        own = jnp.where(same, sacc[g], 0.0)
-        wide = jnp.dot(own, gather, precision=high, preferred_element_type=F32)
-        wide = jnp.where(inner, wide, 0.0)
-        share = jnp.dot(pick, wide, precision=high, preferred_element_type=F32)
-        sec_send[:, g] = share.reshape(DP, G, 128)
+        for d in range(DP):
+            sec_send[d, 4 * g : 4 * g + 4] = sacc[g, 4 * d : 4 * d + 4]
 
     def s_copy(p):
         t = (dp + p) % DP
@@ -223,6 +235,7 @@
 
     for p in range(1, DP):
         s_copy(p).start()
+    gate_part(CHUNKS - 1)
 
     def drain(k, carry):
         wait_sent(h_send, k, h_ss)
@@ -234,6 +247,29 @@
         s_copy(p).wait()
         total = total + sec_recv[p - 1]
     so[...] = total * scale
+
+
+def write_out(ig, gg, fo, so, ig_out, gg_out, fo_out, so_out, sem):
+    rows = ig.shape[0] // 2
+    copies = [pltpu.make_async_copy(fo, fo_out, sem.at[4])]
+    for a in range(2):
+        part = pl.ds(a * rows, rows)
+        copies.append(pltpu.make_async_copy(ig.at[part], ig_out.at[part], sem.at[a]))
+        copies.append(pltpu.make_async_copy(gg.at[part], gg_out.at[part], sem.at[2 + a]))
+    for copy in copies:
+        copy.start()
+    n = G * NB
+    gather = (iota((n, NB), 0) // G == iota((n, NB), 1)).astype(F32)
+    own = iota((G, 4, n), 0) == iota((G, 4, n), 2) % G
+    for g in range(2):
+        wide = jnp.where(own, so[4 * g : 4 * g + 4][None], 0.0).reshape(G * 4, n)
+        share = jnp.dot(
+            wide, gather, precision=lax.Precision.HIGHEST, preferred_element_type=F32
+        )
+        for i in range(G):
+            so_out[g * G + i] = share[4 * i : 4 * i + 4]
+    for copy in copies:
+        copy.wait()
 
 
 def local(tokens, gate, cotangent, first_factor, second_factor):
@@ -244,7 +280,7 @@
     vm = pltpu.VMEM
     dma = pltpu.SemaphoreType.DMA
     out = (
-        vm(flat, BF16), vm(flat, BF16), vm((2, 64, BS), F32), vm((2, G, 128), F32),
+        vm(flat, BF16), vm(flat, BF16), vm((2, 64, BS), F32), vm((8, G * NB), F32),
     )
     scratch = [
         vm((CHUNKS, rows, cw), BF16), vm((CHUNKS, rows, cw), BF16), vm((CHUNKS, rows, cw), BF16),
@@ -252,9 +288,9 @@
         vm((2, BS, BS), BF16), vm((2, BS, BS), BF16),
         vm((CHUNKS, SEQ, 2, 2, G, cw), BF16), vm((CHUNKS, SEQ, 2, 2, G, cw), BF16),
         vm((CHUNKS, 2, NB, G, cw), BF16), vm((CHUNKS, 2, NB, G, cw), BF16),
-        vm((2, 4, 2, 64, BS), F32), vm((2, BS, BS), F32), vm((3, 2, 2, 64, BS), F32),
+        vm((2, 4, 2, 64, BS), F32), vm((2, NB, G * NB), F32), vm((3, 2, 2, 64, BS), F32),
         vm((2, 64, BS), BF16), vm((2, 64, BS), BF16), vm((2, 64, BS), F32),
-        vm((DP, 2, G, 128), F32), vm((DP - 1, 2, G, 128), F32),
+        vm((DP, 8, G * NB), F32), vm((DP - 1, 8, G * NB), F32),
         dma((3, CHUNKS)), dma((2,)),
         dma((CHUNKS,)), dma((CHUNKS,)), dma((CHUNKS,)), dma((CHUNKS,)),
         dma((3,)), dma((3,)), dma, dma, dma((DP - 1,)), dma((DP - 1,)),
@@ -278,10 +314,19 @@
         tokens.reshape(flat), gate.reshape(flat), cotangent.reshape(flat),
         first_factor, second_factor.reshape(BS * 2, NB),
     )
-    return (
-        ig.reshape(seqs, rows, width), gg.reshape(seqs, rows, width),
-        fo, so.reshape(NB, 4, NB),
-    )
+    ig, gg, fo, so = pl.pallas_call(
+        write_out,
+        out_shape=(
+            jax.ShapeDtypeStruct(flat, BF16), jax.ShapeDtypeStruct(flat, BF16),
+            jax.ShapeDtypeStruct((2, 64, BS), F32), jax.ShapeDtypeStruct((NB, 4, NB), F32),
+        ),
+        in_specs=[inner] * 4,
+        out_specs=[hbm] * 3 + [inner],
+        scratch_shapes=[dma((5,))],
+        compiler_params=pltpu.CompilerParams(vmem_limit_bytes=8 * 2**20),
+        name="write_out",
+    )(ig, gg, fo, so)
+    return (ig.reshape(seqs, rows, width), gg.reshape(seqs, rows, width), fo, so)
 
 
 def solution(mesh):

time: 120 us -> 114 us (0.950)
  local copies, waits for them, and re-layouts: 5.45 us -> 0 us
    unnamed x3 -> x0, local copies, waits for them, and re-layouts: 4.73 us -> none
    pallas_call x1, Pallas kernels: 113 us -> 109 us  [local(): pl.pallas_call(functools.partial(kernel, width, scale), out_shape=out, in...]
    pallas_call x0 -> x1, Pallas kernels: none -> 4.09 us  [local(): pl.pallas_call(write_out, out_shape=(jax.ShapeDtypeStruct(flat, BF16), ja...]
where the time goes in v2:
time: 114 us; the launch traced here: 113 us
  Pallas kernels  113 us (99%)
    pallas_call x1, Pallas kernels, local(): pl.pallas_call(functools.partial(kernel, width, scale), out_shape=out, in...  109 us
    pallas_call x1, Pallas kernels, local(): pl.pallas_call(write_out, out_shape=(jax.ShapeDtypeStruct(flat, BF16), ja...  4.09 us

profile of v2, /device:TPU:1, one launch (start us, length us, event | category | flops | bytes accessed | tf_op | source)
XLA Modules:
  0.0 113.2 jit_solution(6833472129232160859)
XLA Ops:
  0.6 108.5 %mixer.1 = (bf16[1024,2048]{1,0:T(8,128)(2,1)S(1)}, bf16[1024,2048]{1,0:T(8,128)(2,1)S(1)}, f32[2,64,512]{2,1,0:T(8,128)S(1)}, f32[8,512]{1,0:T(8,128)S(1)}) custom-call(bf16[1024,2048]{1,0:T(8,128)(2,1)} %bitcast.6, bf16[1024,2048]{1,0:T(8,128)(2,1)} %bitcast.7, bf16[1024,2048]{1,0:T(8,128)(2,1)} %bitcast.8, bf16[2,512,512]{2,1,0:T(8,128)(2,1)} %first.1, ...), custom_call_target="tpu_custom_call" | custom-call | flops 16106127360 | bytes 23068672 | tf_op jit(solution)/shard_map/mixer/pallas_call | solution.py:300
  109.2 4.1 %write_out.1 = (bf16[1024,2048]{1,0:T(8,128)(2,1)}, bf16[1024,2048]{1,0:T(8,128)(2,1)}, f32[2,64,512]{2,1,0:T(8,128)}, f32[32,4,32]{2,1,0:T(4,128)}) custom-call(bf16[1024,2048]{1,0:T(8,128)(2,1)S(1)} %get-tuple-element.12.ig, bf16[1024,2048]{1,0:T(8,128)(2,1)S(1)} %get-tuple-element.13.gg, f32[2,64,512]{2,1,0:T(8,128)S(1)} %get-tuple-element.14.fo, ...), custom_call_target="tpu_custom_call" | custom-call | tf_op jit(solution)/shard_map/write_out/pallas_call | solution.py:317

commit v3 on v2

--- a/solution.py
+++ b/solution.py
@@ -10,7 +10,7 @@
 
 MESH = pl.DeviceIdType.MESH
 F32, BF16 = jnp.float32, jnp.bfloat16
-CHUNKS = 8
+CHUNKS = 16
 SEQ, DP = 16, 8
 NB, BS, G = 32, 512, 16
 NT = (((1,), (1,)), ((), ()))
@@ -51,6 +51,8 @@
 
     load_second = pltpu.make_async_copy(second, s_v, fac_sem.at[0])
     load_first = pltpu.make_async_copy(first, f_v, fac_sem.at[1])
+    load_first.start()
+    start_loads(0, (2,))
     load_second.start()
     start_loads(0, (0, 1))
 
@@ -66,6 +68,38 @@
 
     lax.fori_loop(1, SEQ, greet_seq, 0)
     lax.fori_loop(1, DP, greet_dp, 0)
+
+    def send(src, dst, k, ss, rs):
+        place = dst.at[k, :, pl.ds(2 * me, 2)]
+
+        def one(p, carry):
+            t = (me + p) % SEQ
+            pltpu.make_async_remote_copy(
+                src_ref=src.at[k, t], dst_ref=place, send_sem=ss.at[k], recv_sem=rs.at[k],
+                device_id=(dp, t), device_id_type=MESH,
+            ).start()
+            return carry
+
+        lax.fori_loop(1, SEQ, one, 0)
+        pltpu.make_async_copy(src.at[k, me], place, rs.at[k]).start()
+
+    def wait_sent(src, k, ss):
+        ref = src.at[k, pl.ds(0, SEQ - 1)]
+        pltpu.make_async_copy(ref, ref, ss.at[k]).wait()
+
+    def wait_all(dst, k, rs):
+        pltpu.make_async_copy(dst.at[k], dst.at[k], rs.at[k]).wait()
+
+    def make_h(k):
+        wait_loads(k, (2,))
+        for b in range(2):
+            h = jnp.dot(f_v[b], tok_v[k, b * BS : (b + 1) * BS, :], preferred_element_type=F32)
+            h_send[k, :, :, b] = h.astype(BF16).reshape(SEQ, 2, G, cw)
+
+    load_first.wait()
+    make_h(0)
+    pl.semaphore_wait(barrier, SEQ - 1 + DP - 1)
+    send(h_send, h_recv, 0, h_ss, h_rs)
     start_loads(1, (0, 1))
 
     load_second.wait()
@@ -79,27 +113,6 @@
         )
         wt_v[g] = jnp.where(same_t, wt, 0.0).astype(BF16)
 
-    def send(src, dst, k, ss, rs):
-        place = dst.at[k, :, pl.ds(2 * me, 2)]
-
-        def one(p, carry):
-            t = (me + p) % SEQ
-            pltpu.make_async_remote_copy(
-                src_ref=src.at[k, t], dst_ref=place, send_sem=ss.at[k], recv_sem=rs.at[k],
-                device_id=(dp, t), device_id_type=MESH,
-            ).start()
-            return carry
-
-        lax.fori_loop(1, SEQ, one, 0)
-        pltpu.make_async_copy(src.at[k, me], place, rs.at[k]).start()
-
-    def wait_sent(src, k, ss):
-        ref = src.at[k, pl.ds(0, SEQ - 1)]
-        pltpu.make_async_copy(ref, ref, ss.at[k]).wait()
-
-    def wait_all(dst, k, rs):
-        pltpu.make_async_copy(dst.at[k], dst.at[k], rs.at[k]).wait()
-
     def make_hg(k):
         wait_loads(k, (0, 1))
         for g in range(2):
@@ -109,43 +122,35 @@
             hg = jnp.dot(wt_v[g], m, preferred_element_type=F32).astype(BF16)
             hg_send[k, :, :, g] = hg.reshape(SEQ, 2, G, cw)
 
-    make_hg(0)
-    pl.semaphore_wait(barrier, SEQ - 1 + DP - 1)
-    send(hg_send, hg_recv, 0, hg_ss, hg_rs)
+    start_loads(2, (0, 1))
 
     def hg_step(k, carry):
-        @pl.when(k < CHUNKS - 1)
+        @pl.when(k < CHUNKS - 3)
         def _():
-            start_loads(k + 1, (0, 1))
+            start_loads(k + 3, (0, 1))
 
         make_hg(k)
         send(hg_send, hg_recv, k, hg_ss, hg_rs)
         return carry
 
-    lax.fori_loop(1, CHUNKS, hg_step, 0)
-
-    load_first.start()
+    lax.fori_loop(0, CHUNKS, hg_step, 0)
 
     def load_tok(k, carry):
         start_loads(k, (2,))
         return carry
 
-    lax.fori_loop(0, CHUNKS, load_tok, 0)
+    lax.fori_loop(1, CHUNKS, load_tok, 0)
     for g in range(2):
         w = lax.dot_general(
             s_v[g * n : (g + 1) * n, :], spread, NT, preferred_element_type=F32
         )
         w_v[g] = jnp.where(same, w, 0.0).astype(BF16)
-    load_first.wait()
 
     def h_step(k, carry):
-        wait_loads(k, (2,))
-        for b in range(2):
-            h = jnp.dot(f_v[b], tok_v[k, b * BS : (b + 1) * BS, :], preferred_element_type=F32)
-            h_send[k, :, :, b] = h.astype(BF16).reshape(SEQ, 2, G, cw)
-        return carry
-
-    lax.fori_loop(0, CHUNKS, h_step, 0)
+        make_h(k)
+        return carry
+
+    lax.fori_loop(1, CHUNKS, h_step, 0)
     for b in range(2):
         ft_v[b] = f_v[b].T
 
@@ -154,7 +159,11 @@
 
     def back_step(k, carry):
         wait_sent(hg_send, k, hg_ss)
-        send(h_send, h_recv, k, h_ss, h_rs)
+
+        @pl.when(k < CHUNKS - 1)
+        def _():
+            send(h_send, h_recv, k + 1, h_ss, h_rs)
+
         wait_all(hg_recv, k, hg_rs)
         cols = pl.ds(pl.multiple_of(k * cw, cw), cw)
         for b in range(2):
@@ -217,25 +226,28 @@
         xkeep[b] = facc[b, z, xl] + zrecv[0, b, xl] + zrecv[1, b, xl] + zrecv[2, b, xl]
 
     lax.fori_loop(half, CHUNKS - 1, forth_step, 0)
-    x_copy.wait()
-    fo[...] = (xkeep[...] + xrecv[...].astype(F32)) * scale
     wait_all(h_recv, CHUNKS - 1, h_rs)
     second_terms(CHUNKS - 1)
     for g in range(2):
         for d in range(DP):
             sec_send[d, 4 * g : 4 * g + 4] = sacc[g, 4 * d : 4 * d + 4]
 
+    order = ((2, 1), (1, 1), (3, 1), (2, 0), (1, 0), (3, 0), (0, 1))
+
     def s_copy(p):
-        t = (dp + p) % DP
+        dz, dx = order[p]
+        t = (z + dz) % 4 * 2 + (xl + dx) % 2
         return pltpu.make_async_remote_copy(
-            src_ref=sec_send.at[t], dst_ref=sec_recv.at[p - 1],
-            send_sem=s_ss.at[p - 1], recv_sem=s_rs.at[p - 1],
+            src_ref=sec_send.at[t], dst_ref=sec_recv.at[p],
+            send_sem=s_ss.at[p], recv_sem=s_rs.at[p],
             device_id=(t, me), device_id_type=MESH,
         )
 
-    for p in range(1, DP):
+    for p in range(DP - 1):
         s_copy(p).start()
     gate_part(CHUNKS - 1)
+    x_copy.wait()
+    fo[...] = (xkeep[...] + xrecv[...].astype(F32)) * scale
 
     def drain(k, carry):
         wait_sent(h_send, k, h_ss)
@@ -243,9 +255,9 @@
 
     lax.fori_loop(0, CHUNKS, drain, 0)
     total = sec_send[dp]
-    for p in range(1, DP):
+    for p in reversed(range(DP - 1)):
         s_copy(p).wait()
-        total = total + sec_recv[p - 1]
+        total = total + sec_recv[p]
     so[...] = total * scale
 
 

time: 114 us -> 111 us (0.974)
  Pallas kernels: 113 us -> 110 us
    pallas_call x1, Pallas kernels: 109 us -> 106 us  [local(): pl.pallas_call(functools.partial(kernel, width, scale), out_shape=out, in...]
where the time goes in v3:
time: 111 us
  Pallas kernels  110 us (99%)
    pallas_call x1, Pallas kernels, local(): pl.pallas_call(functools.partial(kernel, width, scale), out_shape=out, in...  106 us
    pallas_call x1, Pallas kernels, local(): pl.pallas_call(write_out, out_shape=(jax.ShapeDtypeStruct(flat, BF16), ja...  4.09 us

profile of v3, /device:TPU:1, one launch (start us, length us, event | category | flops | bytes accessed | tf_op | source)
XLA Modules:
  0.0 111.0 jit_solution(8029191714096336490)
XLA Ops:
  0.6 106.3 %mixer.1 = (bf16[1024,2048]{1,0:T(8,128)(2,1)S(1)}, bf16[1024,2048]{1,0:T(8,128)(2,1)S(1)}, f32[2,64,512]{2,1,0:T(8,128)S(1)}, f32[8,512]{1,0:T(8,128)S(1)}) custom-call(bf16[1024,2048]{1,0:T(8,128)(2,1)} %bitcast.6, bf16[1024,2048]{1,0:T(8,128)(2,1)} %bitcast.7, bf16[1024,2048]{1,0:T(8,128)(2,1)} %bitcast.8, bf16[2,512,512]{2,1,0:T(8,128)(2,1)} %first.1, ...), custom_call_target="tpu_custom_call" | custom-call | flops 16106127360 | bytes 23068672 | tf_op jit(solution)/shard_map/mixer/pallas_call | solution.py:312
  106.9 4.1 %write_out.1 = (bf16[1024,2048]{1,0:T(8,128)(2,1)}, bf16[1024,2048]{1,0:T(8,128)(2,1)}, f32[2,64,512]{2,1,0:T(8,128)}, f32[32,4,32]{2,1,0:T(4,128)}) custom-call(bf16[1024,2048]{1,0:T(8,128)(2,1)S(1)} %get-tuple-element.12.ig, bf16[1024,2048]{1,0:T(8,128)(2,1)S(1)} %get-tuple-element.13.gg, f32[2,64,512]{2,1,0:T(8,128)S(1)} %get-tuple-element.14.fo, ...), custom_call_target="tpu_custom_call" | custom-call | tf_op jit(solution)/shard_map/write_out/pallas_call | solution.py:329

commit v4 on v3

--- a/solution.py
+++ b/solution.py
@@ -10,6 +10,7 @@
 
 MESH = pl.DeviceIdType.MESH
 F32, BF16 = jnp.float32, jnp.bfloat16
+WINDOW = 16
 CHUNKS = 16
 SEQ, DP = 16, 8
 NB, BS, G = 32, 512, 16
@@ -70,7 +71,7 @@
     lax.fori_loop(1, DP, greet_dp, 0)
 
     def send(src, dst, k, ss, rs):
-        place = dst.at[k, :, pl.ds(2 * me, 2)]
+        place = dst.at[k, me]
 
         def one(p, carry):
             t = (me + p) % SEQ
@@ -124,16 +125,50 @@
 
     start_loads(2, (0, 1))
 
-    def hg_step(k, carry):
+    def load_pair(k):
         @pl.when(k < CHUNKS - 3)
         def _():
             start_loads(k + 3, (0, 1))
 
+    def hg_first(k, carry):
+        load_pair(k)
         make_hg(k)
         send(hg_send, hg_recv, k, hg_ss, hg_rs)
         return carry
 
-    lax.fori_loop(0, CHUNKS, hg_step, 0)
+    def hg_rest(k, carry):
+        load_pair(k)
+        make_hg(k)
+        return carry
+
+    lax.fori_loop(0, WINDOW - 1, hg_first, 0)
+    lax.fori_loop(WINDOW - 1, CHUNKS, hg_rest, 0)
+
+    def start_item(n):
+        @pl.when(n <= CHUNKS)
+        def _():
+            send(hg_send, hg_recv, n - 1, hg_ss, hg_rs)
+
+        @pl.when((n > CHUNKS) & (n < 2 * CHUNKS))
+        def _():
+            send(h_send, h_recv, n - CHUNKS, h_ss, h_rs)
+
+    def wait_item(n):
+        @pl.when((n > 0) & (n <= CHUNKS))
+        def _():
+            wait_sent(hg_send, n - 1, hg_ss)
+
+        @pl.when(n > CHUNKS)
+        def _():
+            wait_sent(h_send, n - CHUNKS, h_ss)
+
+        @pl.when(n == 0)
+        def _():
+            wait_sent(h_send, 0, h_ss)
+
+    def next_item(n):
+        wait_item(n)
+        start_item(n + WINDOW)
 
     def load_tok(k, carry):
         start_loads(k, (2,))
@@ -158,16 +193,11 @@
     sacc[...] = jnp.zeros_like(sacc)
 
     def back_step(k, carry):
-        wait_sent(hg_send, k, hg_ss)
-
-        @pl.when(k < CHUNKS - 1)
-        def _():
-            send(h_send, h_recv, k + 1, h_ss, h_rs)
-
+        next_item(k)
         wait_all(hg_recv, k, hg_rs)
         cols = pl.ds(pl.multiple_of(k * cw, cw), cw)
         for b in range(2):
-            hg = hg_recv[k, b].reshape(BS, cw)
+            hg = hg_recv[k, :, b].reshape(BS, cw)
             rows = slice(b * BS, (b + 1) * BS)
             ig[rows, cols] = jnp.dot(ft_v[b], hg, preferred_element_type=F32).astype(BF16)
             terms = lax.dot_general(hg, tok_v[k, rows, :], NT, preferred_element_type=F32)
@@ -193,7 +223,7 @@
 
     def second_terms(k):
         for g in range(2):
-            h = h_recv[k, g].reshape(n, cw)
+            h = h_recv[k, :, g].reshape(n, cw)
             m = mg_v[k, g * n : (g + 1) * n, :]
             terms = lax.dot_general(m, h, NT, preferred_element_type=F32)
             terms = jnp.where(same, terms, 0.0).reshape(G, NB, n)
@@ -202,12 +232,13 @@
     def gate_part(k):
         cols = pl.ds(pl.multiple_of(k * cw, cw), cw)
         for g in range(2):
-            h = h_recv[k, g].reshape(n, cw)
+            h = h_recv[k, :, g].reshape(n, cw)
             rows = slice(g * n, (g + 1) * n)
             mixed = jnp.dot(w_v[g], h, preferred_element_type=F32)
             gg[rows, cols] = (cot_v[k, rows, :].astype(F32) * mixed).astype(BF16)
 
     def forth_step(k, carry):
+        next_item(k + CHUNKS)
         wait_all(h_recv, k, h_rs)
         second_terms(k)
         gate_part(k)
@@ -249,11 +280,7 @@
     x_copy.wait()
     fo[...] = (xkeep[...] + xrecv[...].astype(F32)) * scale
 
-    def drain(k, carry):
-        wait_sent(h_send, k, h_ss)
-        return carry
-
-    lax.fori_loop(0, CHUNKS, drain, 0)
+    wait_item(2 * CHUNKS - 1)
     total = sec_send[dp]
     for p in reversed(range(DP - 1)):
         s_copy(p).wait()
@@ -261,7 +288,7 @@
     so[...] = total * scale
 
 
-def write_out(ig, gg, fo, so, ig_out, gg_out, fo_out, so_out, sem):
+def write_out(ig, gg, fo, so, ig_out, gg_out, fo_out, so_out, so_v, sem):
     rows = ig.shape[0] // 2
     copies = [pltpu.make_async_copy(fo, fo_out, sem.at[4])]
     for a in range(2):
@@ -279,7 +306,9 @@
             wide, gather, precision=lax.Precision.HIGHEST, preferred_element_type=F32
         )
         for i in range(G):
-            so_out[g * G + i] = share[4 * i : 4 * i + 4]
+            so_v[g * G + i] = share[4 * i : 4 * i + 4]
+    copies.append(pltpu.make_async_copy(so_v, so_out, sem.at[5]))
+    copies[-1].start()
     for copy in copies:
         copy.wait()
 
@@ -299,7 +328,7 @@
         vm((2, BS, BS), BF16), vm((2, BS, BS), BF16), vm((BS * 2, NB), BF16),
         vm((2, BS, BS), BF16), vm((2, BS, BS), BF16),
         vm((CHUNKS, SEQ, 2, 2, G, cw), BF16), vm((CHUNKS, SEQ, 2, 2, G, cw), BF16),
-        vm((CHUNKS, 2, NB, G, cw), BF16), vm((CHUNKS, 2, NB, G, cw), BF16),
+        vm((CHUNKS, SEQ, 2, 2, G, cw), BF16), vm((CHUNKS, SEQ, 2, 2, G, cw), BF16),
         vm((2, 4, 2, 64, BS), F32), vm((2, NB, G * NB), F32), vm((3, 2, 2, 64, BS), F32),
         vm((2, 64, BS), BF16), vm((2, 64, BS), BF16), vm((2, 64, BS), F32),
         vm((DP, 8, G * NB), F32), vm((DP - 1, 8, G * NB), F32),
@@ -333,8 +362,8 @@
             jax.ShapeDtypeStruct((2, 64, BS), F32), jax.ShapeDtypeStruct((NB, 4, NB), F32),
         ),
         in_specs=[inner] * 4,
-        out_specs=[hbm] * 3 + [inner],
-        scratch_shapes=[dma((5,))],
+        out_specs=[hbm] * 4,
+        scratch_shapes=[vm((NB, 4, NB), F32), dma((6,))],
         compiler_params=pltpu.CompilerParams(vmem_limit_bytes=8 * 2**20),
         name="write_out",
     )(ig, gg, fo, so)

time: 111 us -> 111 us (level)
  no operation moved by 1% of the time
where the time goes in v4:
time: 111 us; the launch traced here: 110 us
  Pallas kernels  110 us (99%)
    pallas_call x1, Pallas kernels, local(): pl.pallas_call(functools.partial(kernel, width, scale), out_shape=out, in...  106 us
    pallas_call x1, Pallas kernels, local(): pl.pallas_call(write_out, out_shape=(jax.ShapeDtypeStruct(flat, BF16), ja...  3.47 us

profile of v4, /device:TPU:1, one launch (start us, length us, event | category | flops | bytes accessed | tf_op | source)
XLA Modules:
  0.0 110.4 jit_solution(16533159055338796783)
XLA Ops:
  0.6 106.3 %mixer.1 = (bf16[1024,2048]{1,0:T(8,128)(2,1)S(1)}, bf16[1024,2048]{1,0:T(8,128)(2,1)S(1)}, f32[2,64,512]{2,1,0:T(8,128)S(1)}, f32[8,512]{1,0:T(8,128)S(1)}) custom-call(bf16[1024,2048]{1,0:T(8,128)(2,1)} %bitcast.6, bf16[1024,2048]{1,0:T(8,128)(2,1)} %bitcast.7, bf16[1024,2048]{1,0:T(8,128)(2,1)} %bitcast.8, bf16[2,512,512]{2,1,0:T(8,128)(2,1)} %first.1, ...), custom_call_target="tpu_custom_call" | custom-call | flops 16106127360 | bytes 23068672 | tf_op jit(solution)/shard_map/mixer/pallas_call | solution.py:341
  106.9 3.5 %write_out.1 = (bf16[1024,2048]{1,0:T(8,128)(2,1)}, bf16[1024,2048]{1,0:T(8,128)(2,1)}, f32[2,64,512]{2,1,0:T(8,128)}, f32[32,4,32]{2,1,0:T(4,128)}) custom-call(bf16[1024,2048]{1,0:T(8,128)(2,1)S(1)} %get-tuple-element.12.ig, bf16[1024,2048]{1,0:T(8,128)(2,1)S(1)} %get-tuple-element.13.gg, f32[2,64,512]{2,1,0:T(8,128)S(1)} %get-tuple-element.14.fo, ...), custom_call_target="tpu_custom_call" | custom-call | tf_op jit(solution)/shard_map/write_out/pallas_call | solution.py:358

commit v5 on v4

--- a/solution.py
+++ b/solution.py
@@ -237,32 +237,6 @@
             mixed = jnp.dot(w_v[g], h, preferred_element_type=F32)
             gg[rows, cols] = (cot_v[k, rows, :].astype(F32) * mixed).astype(BF16)
 
-    def forth_step(k, carry):
-        next_item(k + CHUNKS)
-        wait_all(h_recv, k, h_rs)
-        second_terms(k)
-        gate_part(k)
-        return carry
-
-    half = CHUNKS // 2
-    lax.fori_loop(0, half, forth_step, 0)
-
-    for d in (1, 2, 3):
-        z_copy(d).wait()
-    for b in range(2):
-        other = facc[b, z, 1 - xl] + zrecv[0, b, 1 - xl] + zrecv[1, b, 1 - xl] + zrecv[2, b, 1 - xl]
-        xsend[b] = other.astype(BF16)
-    x_copy.start()
-    for b in range(2):
-        xkeep[b] = facc[b, z, xl] + zrecv[0, b, xl] + zrecv[1, b, xl] + zrecv[2, b, xl]
-
-    lax.fori_loop(half, CHUNKS - 1, forth_step, 0)
-    wait_all(h_recv, CHUNKS - 1, h_rs)
-    second_terms(CHUNKS - 1)
-    for g in range(2):
-        for d in range(DP):
-            sec_send[d, 4 * g : 4 * g + 4] = sacc[g, 4 * d : 4 * d + 4]
-
     order = ((2, 1), (1, 1), (3, 1), (2, 0), (1, 0), (3, 0), (0, 1))
 
     def s_copy(p):
@@ -274,9 +248,33 @@
             device_id=(t, me), device_id_type=MESH,
         )
 
-    for p in range(DP - 1):
-        s_copy(p).start()
-    gate_part(CHUNKS - 1)
+    def sum_z():
+        for d in (1, 2, 3):
+            z_copy(d).wait()
+        for b in range(2):
+            other = facc[b, z, 1 - xl] + zrecv[0, b, 1 - xl] + zrecv[1, b, 1 - xl] + zrecv[2, b, 1 - xl]
+            xsend[b] = other.astype(BF16)
+        x_copy.start()
+        for b in range(2):
+            xkeep[b] = facc[b, z, xl] + zrecv[0, b, xl] + zrecv[1, b, xl] + zrecv[2, b, xl]
+
+    def share_second():
+        for g in range(2):
+            for d in range(DP):
+                sec_send[d, 4 * g : 4 * g + 4] = sacc[g, 4 * d : 4 * d + 4]
+        for p in range(DP - 1):
+            s_copy(p).start()
+
+    def forth_step(k, carry):
+        pl.when(k < CHUNKS - 1)(lambda: next_item(k + CHUNKS))
+        wait_all(h_recv, k, h_rs)
+        second_terms(k)
+        pl.when(k == CHUNKS // 2)(sum_z)
+        pl.when(k == CHUNKS - 1)(share_second)
+        gate_part(k)
+        return carry
+
+    lax.fori_loop(0, CHUNKS, forth_step, 0)
     x_copy.wait()
     fo[...] = (xkeep[...] + xrecv[...].astype(F32)) * scale
 

time: 111 us -> 111 us (level)
  no operation moved by 1% of the time
where the time goes in v5:
time: 111 us; the launch traced here: 110 us
  Pallas kernels  110 us (99%)
    pallas_call x1, Pallas kernels, local(): pl.pallas_call(functools.partial(kernel, width, scale), out_shape=out, in...  106 us
    pallas_call x1, Pallas kernels, local(): pl.pallas_call(write_out, out_shape=(jax.ShapeDtypeStruct(flat, BF16), ja...  3.47 us

profile of v5, /device:TPU:1, one launch (start us, length us, event | category | flops | bytes accessed | tf_op | source)
XLA Modules:
  0.0 110.4 jit_solution(16958249286075239631)
XLA Ops:
  0.6 106.3 %mixer.1 = (bf16[1024,2048]{1,0:T(8,128)(2,1)S(1)}, bf16[1024,2048]{1,0:T(8,128)(2,1)S(1)}, f32[2,64,512]{2,1,0:T(8,128)S(1)}, f32[8,512]{1,0:T(8,128)S(1)}) custom-call(bf16[1024,2048]{1,0:T(8,128)(2,1)} %bitcast.6, bf16[1024,2048]{1,0:T(8,128)(2,1)} %bitcast.7, bf16[1024,2048]{1,0:T(8,128)(2,1)} %bitcast.8, bf16[2,512,512]{2,1,0:T(8,128)(2,1)} %first.1, ...), custom_call_target="tpu_custom_call" | custom-call | flops 16106127360 | bytes 23068672 | tf_op jit(solution)/shard_map/mixer/pallas_call | solution.py:339
  106.9 3.5 %write_out.1 = (bf16[1024,2048]{1,0:T(8,128)(2,1)}, bf16[1024,2048]{1,0:T(8,128)(2,1)}, f32[2,64,512]{2,1,0:T(8,128)}, f32[32,4,32]{2,1,0:T(4,128)}) custom-call(bf16[1024,2048]{1,0:T(8,128)(2,1)S(1)} %get-tuple-element.12.ig, bf16[1024,2048]{1,0:T(8,128)(2,1)S(1)} %get-tuple-element.13.gg, f32[2,64,512]{2,1,0:T(8,128)S(1)} %get-tuple-element.14.fo, ...), custom_call_target="tpu_custom_call" | custom-call | tf_op jit(solution)/shard_map/write_out/pallas_call | solution.py:356

commit v6 on v5

--- a/solution.py
+++ b/solution.py
@@ -27,7 +27,7 @@
     ig, gg, fo, so,
     tok_v, cot_v, mg_v, f_v, ft_v, s_v, w_v, wt_v,
     hg_send, h_send, hg_recv, h_recv,
-    facc, sacc, zrecv, xsend, xrecv, xkeep, sec_send, sec_recv,
+    facc, sacc, zrecv, xsend, xrecv, xkeep, sec_own, sec_send, sec_recv,
     load_sem, fac_sem, hg_ss, hg_rs, h_ss, h_rs, z_ss, z_rs, x_ss, x_rs, s_ss, s_rs,
 ):
     cw = width // CHUNKS
@@ -259,9 +259,11 @@
             xkeep[b] = facc[b, z, xl] + zrecv[0, b, xl] + zrecv[1, b, xl] + zrecv[2, b, xl]
 
     def share_second():
-        for g in range(2):
-            for d in range(DP):
-                sec_send[d, 4 * g : 4 * g + 4] = sacc[g, 4 * d : 4 * d + 4]
+        for d in range(DP):
+            part = jnp.concatenate([sacc[0, 4 * d : 4 * d + 4], sacc[1, 4 * d : 4 * d + 4]], axis=0)
+            part = jnp.concatenate([part[:, : n // 2], part[:, n // 2 :]], axis=0)
+            sec_own[d] = part
+            sec_send[d] = part.astype(BF16)
         for p in range(DP - 1):
             s_copy(p).start()
 
@@ -279,11 +281,12 @@
     fo[...] = (xkeep[...] + xrecv[...].astype(F32)) * scale
 
     wait_item(2 * CHUNKS - 1)
-    total = sec_send[dp]
+    total = sec_own[dp]
     for p in reversed(range(DP - 1)):
         s_copy(p).wait()
-        total = total + sec_recv[p]
-    so[...] = total * scale
+        total = total + sec_recv[p].astype(F32)
+    so[:, : n // 2] = total[:8] * scale
+    so[:, n // 2 :] = total[8:] * scale
 
 
 def write_out(ig, gg, fo, so, ig_out, gg_out, fo_out, so_out, so_v, sem):
@@ -329,7 +332,7 @@
         vm((CHUNKS, SEQ, 2, 2, G, cw), BF16), vm((CHUNKS, SEQ, 2, 2, G, cw), BF16),
         vm((2, 4, 2, 64, BS), F32), vm((2, NB, G * NB), F32), vm((3, 2, 2, 64, BS), F32),
         vm((2, 64, BS), BF16), vm((2, 64, BS), BF16), vm((2, 64, BS), F32),
-        vm((DP, 8, G * NB), F32), vm((DP - 1, 8, G * NB), F32),
+        vm((DP, 16, G * NB // 2), F32), vm((DP, 16, G * NB // 2), BF16), vm((DP - 1, 16, G * NB // 2), BF16),
         dma((3, CHUNKS)), dma((2,)),
         dma((CHUNKS,)), dma((CHUNKS,)), dma((CHUNKS,)), dma((CHUNKS,)),
         dma((3,)), dma((3,)), dma, dma, dma((DP - 1,)), dma((DP - 1,)),

time: 111 us -> 110 us (level)
  no operation moved by 1% of the time
where the time goes in v6:
time: 110 us
  Pallas kernels  110 us (100%)
    pallas_call x1, Pallas kernels, local(): pl.pallas_call(functools.partial(kernel, width, scale), out_shape=out, in...  106 us
    pallas_call x1, Pallas kernels, local(): pl.pallas_call(write_out, out_shape=(jax.ShapeDtypeStruct(flat, BF16), ja...  3.47 us

profile of v6, /device:TPU:1, one launch (start us, length us, event | category | flops | bytes accessed | tf_op | source)
XLA Modules:
  0.0 110.2 jit_solution(12360344882828883843)
XLA Ops:
  0.6 106.1 %mixer.1 = (bf16[1024,2048]{1,0:T(8,128)(2,1)S(1)}, bf16[1024,2048]{1,0:T(8,128)(2,1)S(1)}, f32[2,64,512]{2,1,0:T(8,128)S(1)}, f32[8,512]{1,0:T(8,128)S(1)}) custom-call(bf16[1024,2048]{1,0:T(8,128)(2,1)} %bitcast.6, bf16[1024,2048]{1,0:T(8,128)(2,1)} %bitcast.7, bf16[1024,2048]{1,0:T(8,128)(2,1)} %bitcast.8, bf16[2,512,512]{2,1,0:T(8,128)(2,1)} %first.1, ...), custom_call_target="tpu_custom_call" | custom-call | flops 16106127360 | bytes 23068672 | tf_op jit(solution)/shard_map/mixer/pallas_call | solution.py:342
  106.7 3.5 %write_out.1 = (bf16[1024,2048]{1,0:T(8,128)(2,1)}, bf16[1024,2048]{1,0:T(8,128)(2,1)}, f32[2,64,512]{2,1,0:T(8,128)}, f32[32,4,32]{2,1,0:T(4,128)}) custom-call(bf16[1024,2048]{1,0:T(8,128)(2,1)S(1)} %get-tuple-element.12.ig, bf16[1024,2048]{1,0:T(8,128)(2,1)S(1)} %get-tuple-element.13.gg, f32[2,64,512]{2,1,0:T(8,128)S(1)} %get-tuple-element.14.fo, ...), custom_call_target="tpu_custom_call" | custom-call | tf_op jit(solution)/shard_map/write_out/pallas_call | solution.py:359
